TPU v7x, 32 devices: a whole 2x2x4 slice. The times are simulated.
32 devices in a mesh: row: 4 (over x, core), col: 8 (over z, y).
Axes of the slice: x: 2, y: 2, z: 4, core: 2. Of those that a mesh axis runs over, the one named last changes fastest.
Arguments:
- strip_factors: bfloat16 [16384, 64], P(('row', 'col')), may hold values from -8 to 8
- sku_factors: bfloat16 [16384, 64], P('col', 'row'), may hold values from -8 to 8
- probe: bfloat16 [16384, 16], P('col', 'row'), may hold values from -6 to 6
- demand_weight: float32 [1, 16384], P(None, ('row', 'col')), may hold values from 1 to 30, as said below
Outputs:
- basis: float32 [16, 16384], P(None, ('row', 'col'))
Inputs may be any that keep to these rules, and one draw needn't show every extreme that they name: `demand_weight`: positive weights.
All inputs are finite; a program needn't handle non-finite values.
Results may differ from a plain program's by a relative error of at most 0.009.
The roundings to bfloat16 on the way count: a program that leaves them out, or rounds other values in their place, can miss the bound.
Values may be sent and summed in bfloat16 or wider, within the bound.
A program may use at most 64 MiB of HBM per device.

v0:
```python
import jax
import jax.numpy as jnp
from jax import lax
from jax.sharding import PartitionSpec as P


def unit_rows(factors):
    wide = factors.astype(jnp.float32)
    scale = lax.rsqrt(jnp.sum(wide * wide, axis=1, keepdims=True) + 1e-06)
    return (wide * scale).astype(jnp.bfloat16)


def per_device(strip_factors, sku_factors, probe, demand_weight):
    strip_unit = unit_rows(strip_factors)
    panel_raw, probe_cols = (
        lax.all_gather(sku_factors, "row", axis=1, tiled=True),
        lax.all_gather(probe, "row", axis=1, tiled=True),
    )
    sku_unit = unit_rows(panel_raw)
    columns = sku_unit.shape[0]
    width = min(512, columns)
    count = columns // width
    piece = lax.all_gather(strip_unit, "col", axis=0, tiled=True)
    total = jnp.zeros((probe_cols.shape[1], piece.shape[0]), jnp.float32)
    for number in range(count):
        panel = sku_unit[number * width : (number + 1) * width]
        block_probe = probe_cols[number * width : (number + 1) * width]
        corr = lax.dot_general(
            piece, panel, (((1,), (1,)), ((), ())), preferred_element_type=jnp.float32
        )
        affinity = jnp.exp(corr).astype(jnp.bfloat16)
        total = total + lax.dot_general(
            block_probe, affinity, (((0,), (1,)), ((), ())), preferred_element_type=jnp.float32
        )
    image = lax.psum_scatter(total, "col", scatter_dimension=1, tiled=True)
    local_gram = jnp.dot(image * demand_weight, image.T, precision=lax.Precision.HIGHEST)
    gram = lax.psum(local_gram, ("row", "col"))
    lower = jnp.linalg.cholesky(gram)
    return jax.scipy.linalg.solve_triangular(lower, image, lower=True)


def solution(mesh):
    placed = (P(("row", "col"), None), P("col", "row"), P("col", "row"), P(None, ("row", "col")))
    return jax.shard_map(
        per_device, mesh=mesh, in_specs=placed, out_specs=P(None, ("row", "col")), check_vma=False
    )
```

profile of v0, /device:TPU:0, one launch (start us, length us, event | category | flops | bytes accessed | tf_op | source)
XLA Modules:
  0.0 179.3 jit_solution(10715148709017527640)
XLA Ops:
  6.5 0.0 reduce-scatter.2.cloned.1.call-start
  6.5 0.9 fusion.4
  7.4 0.9 fusion.5
  8.3 6.4 %all-gather = bf16[4,4,2048]{2,1,0:T(4,128)(2,1)S(1)} all-gather(bf16[1,4,2048]{2,1,0:T(4,128)(2,1)} %bitcast.26), channel_id=1, replica_groups=mesh['row'=4,'col'=8] {'row'}, dimensions={0}, use_global_device_ids=true | all-gather | bytes 81920 | tf_op jit(solution)/shard_map/all_gather | solution.py:17
  14.7 6.4 %all_gather.10 = bf16[2048,64]{0,1:T(8,128)(2,1)S(1)} all-gather(bf16[2048,16]{0,1:T(8,128)(2,1)} %param.5), channel_id=1, replica_groups=mesh['row'=4,'col'=8] {'row'}, dimensions={1}, use_global_device_ids=true | all-gather | bytes 327680 | tf_op jit(solution)/shard_map/all_gather | solution.py:16
  21.2 0.1 fusion.2
  21.3 32.0 %all_gather.9 = bf16[4096,64]{0,1:T(8,128)(2,1)S(1)} all-gather(bf16[512,64]{0,1:T(8,128)(2,1)S(1)} %fusion.5), channel_id=1, replica_groups=mesh['row'=4,'col'=8] {'col'}, dimensions={0}, use_global_device_ids=true | all-gather | bytes 589824 | tf_op jit(solution)/shard_map/all_gather | solution.py:23
  53.3 2.3 %fusion.1 = f32[4096,16]{0,1:T(8,128)S(1)} fusion(bf16[4096,64]{0,1:T(8,128)(2,1)S(1)} %all_gather.9, bf16[2048,64]{0,1:T(8,128)(2,1)S(1)} %fusion.3, bf16[2048,16]{0,1:T(8,128)(2,1)S(1)} %bitcast.22), kind=kOutput, calls=%fused_computation.8 | convolution fusion | flops 337641472 | bytes 868352 | tf_op jit(solution)/shard_map/dot_general | solution.py:32
  55.7 2.4 %convolution_add_fusion.2 = f32[4096,16]{0,1:T(8,128)S(1)} fusion(f32[4096,16]{0,1:T(8,128)S(1)} %fusion.1, bf16[4096,64]{0,1:T(8,128)(2,1)S(1)} %all_gather.9, bf16[2048,64]{0,1:T(8,128)(2,1)S(1)} %fusion.3, bf16[2048,16]{0,1:T(8,128)(2,1)S(1)} %bitcast.23), kind=kOutput, calls=%fused_computation.7 | convolution fusion | flops 337707008 | bytes 1130496 | tf_op jit(solution)/shard_map/dot_general | solution.py:32
  58.0 2.3 %convolution_add_fusion.1 = f32[4096,16]{0,1:T(8,128)S(1)} fusion(f32[4096,16]{0,1:T(8,128)S(1)} %convolution_add_fusion.2, bf16[4096,64]{0,1:T(8,128)(2,1)S(1)} %all_gather.9, bf16[2048,64]{0,1:T(8,128)(2,1)S(1)} %fusion.3, bf16[2048,16]{0,1:T(8,128)(2,1)S(1)} %bitcast.24), kind=kOutput, calls=%fused_computation.6 | convolution fusion | flops 337707008 | bytes 1130496 | tf_op jit(solution)/shard_map/dot_general | solution.py:32
  60.4 0.0 copy-start
  60.4 3.1 %fusion = f32[16,4096]{1,0:T(8,128)} fusion(f32[4096,16]{0,1:T(8,128)S(1)} %convolution_add_fusion.1, bf16[4096,64]{0,1:T(8,128)(2,1)S(1)} %all_gather.9, bf16[2048,64]{0,1:T(8,128)(2,1)S(1)} %fusion.3, bf16[2048,16]{0,1:T(8,128)(2,1)S(1)} %bitcast.25), kind=kOutput, calls=%fused_computation.5 | convolution fusion | flops 337707008 | bytes 1130496 | tf_op jit(solution)/shard_map/dot_general | solution.py:32
  63.4 0.0 reduce-scatter.2.cloned.1.call-update
  63.5 62.1 %reduce-scatter.2.cloned.1.call-done = f32[16,512]{1,0:T(8,128)} async-done(((f32[16,4096]{1,0:T(8,128)}), f32[16,512]{1,0:T(8,128)}) %reduce-scatter.2.cloned.1.call-update) | async-done | bytes 32784 | tf_op jit(solution)/shard_map/reduce_scatter | solution.py:35
  125.6 0.0 copy-done
  125.6 1.0 fusion.14
  126.6 40.2 %psum.7 = f32[16,16]{0,1:T(8,128)S(1)} all-reduce(f32[16,16]{0,1:T(8,128)S(1)} %fusion.14), channel_id=1, replica_groups=mesh['row'=4,'col'=8] {'row','col'}, use_global_device_ids=true, to_apply=%region_3.0 | all-reduce | flops 256 | bytes 2048 | tf_op jit(solution)/shard_map/psum | solution.py:37
  166.8 0.1 copy.8
  166.9 1.5 cholesky.16
  168.4 0.6 compare_reduce_fusion
  169.0 0.6 fusion.21
  169.7 1.2 custom-call.7
  170.9 1.6 fusion.22
  (6 shorter events, 0.1 us)
Async XLA Ops:
  6.5 119.0 %reduce-scatter.2.cloned.1.call-start = ((), (), s32[]{:S(2)}) async-start(), calls=%async_computation.1 | async-start | bytes 294912 | tf_op jit(solution)/shard_map/reduce_scatter | solution.py:35
  60.4 65.2 %copy-start = (f32[1,512]{1,0:T(1,128)S(1)}, f32[1,512]{1,0:T(1,128)}, u32[]{:S(2)}) copy-start(f32[1,512]{1,0:T(1,128)} %param.7) | copy-start | bytes 6148
Sparse Core Ops, SparseCore 0:
  63.6 61.9 reduce-scatter.1
where the time goes:
time: 180 us; the launch traced here: 179 us
  blocking collectives  85.1 us (47%)
  waiting for transfers between devices  62.1 us (34%)
  between operations  13.4 us (7%)
  matrix products  12.7 us (7%)
  other arithmetic  5.87 us (3%)
    reduce_scatter x1, waiting for transfers between devices, per_device(): image = lax.psum_scatter(total, 'col', scatter_dimension=1, tiled=True)  62.1 us
    psum x1, blocking collectives, per_device(): gram = lax.psum(local_gram, ('row', 'col'))  40.2 us
    all_gather x1, blocking collectives, per_device(): piece = lax.all_gather(strip_unit, 'col', axis=0, tiled=True)  32 us
    dot_general x4, matrix products, per_device(): lax.dot_general(block_probe, affinity, (((0,), (1,)), ((), ())), preferre...  10.1 us
    all_gather x1, blocking collectives, per_device(): lax.all_gather(sku_factors, 'row', axis=1, tiled=True)  6.43 us
    all_gather x1, blocking collectives, per_device(): lax.all_gather(probe, 'row', axis=1, tiled=True)  6.43 us
  transfers between devices with their start and end apart: 1, of which 1 were waited for; matrix products, arithmetic and copies ran while one was open for 0% of the time, Pallas kernels for 0%

commit v1 on v0

--- a/solution.py
+++ b/solution.py
@@ -1,7 +1,14 @@
 import jax
 import jax.numpy as jnp
 from jax import lax
+from jax.experimental import pallas as pl
+from jax.experimental.pallas import tpu as pltpu
 from jax.sharding import PartitionSpec as P
+
+ROWS = 4
+LINE = 4
+GROUP = 2 * ROWS
+CHUNK = 512
 
 
 def unit_rows(factors):
@@ -39,8 +46,262 @@
     return jax.scipy.linalg.solve_triangular(lower, image, lower=True)
 
 
+def other(place, step):
+    low = (place % 2 + step % 2) % 2
+    high = (place // 2 + step // 2) % 2
+    return 2 * high + low
+
+
+def remote(source, target, sent, landed, row, col):
+    return pltpu.make_async_remote_copy(
+        src_ref=source,
+        dst_ref=target,
+        send_sem=sent,
+        recv_sem=landed,
+        device_id=(row, col),
+        device_id_type=pl.DeviceIdType.MESH,
+    )
+
+
+def fused(
+    strip_ref, sku_ref, probe_ref, weight_ref, out_ref,
+    raw, probe_raw, probe_stage, probe_wide, full, units, strips, partial, arrived, gram_line, gram_group,
+    sku_sent, sku_landed, probe_sent, probe_landed, strip_sent, strip_landed,
+    pair_sent, pair_landed, twin_sent, twin_landed, image_sent, image_landed,
+    line_sent, line_landed, group_sent, group_landed,
+):
+    row, col = lax.axis_index("row"), lax.axis_index("col")
+    core = row % 2
+    z, y = col // 2, col % 2
+    twin = row + 1 - 2 * core
+    mate = col + 1 - 2 * y
+    part, skus = sku_ref.shape
+    columns = probe_ref.shape[0]
+    factors = ROWS * part
+    block = ROWS * columns
+    half = skus // 2
+    fold = skus // ROWS
+
+    def line_col(place):
+        return place * 2 + y
+
+    barrier = pltpu.get_barrier_semaphore()
+    for step in range(1, ROWS):
+        pl.semaphore_signal(barrier, inc=1, device_id=(other(row, step), col), device_id_type=pl.DeviceIdType.MESH)
+    for step in range(1, LINE):
+        pl.semaphore_signal(barrier, inc=1, device_id=(row, line_col(other(z, step))), device_id_type=pl.DeviceIdType.MESH)
+    for step in range(ROWS):
+        pl.semaphore_signal(barrier, inc=1, device_id=(other(row, step), mate), device_id_type=pl.DeviceIdType.MESH)
+
+    raw[row] = sku_ref[...]
+    for piece in range(ROWS):
+        probe_stage[piece * columns : (piece + 1) * columns, :] = probe_ref[
+            :, piece * fold : (piece + 1) * fold
+        ].astype(jnp.float32)
+    probe_raw[row] = probe_stage[...].astype(jnp.bfloat16)
+    wide = strip_ref[...].astype(jnp.float32)
+    scale = lax.rsqrt(jnp.sum(wide * wide, axis=0, keepdims=True) + 1e-06)
+    strips[z] = (wide * scale).astype(jnp.bfloat16)
+
+    pl.semaphore_wait(barrier, 2 * ROWS + LINE - 2)
+
+    sends = []
+
+    def send(copy):
+        copy.start()
+        sends.append(copy)
+
+    for step in (2, 3, 1):
+        there = other(row, step)
+        send(remote(sku_ref, raw.at[row], sku_sent.at[step], sku_landed.at[row], there, col))
+        send(remote(probe_raw.at[row], probe_raw.at[row], probe_sent.at[step], probe_landed.at[row], there, col))
+    for step in range(1, LINE):
+        there = line_col(other(z, step))
+        send(remote(strips.at[z], strips.at[z], strip_sent.at[step], strip_landed.at[z], row, there))
+
+    for step in range(1, ROWS):
+        there = other(row, step)
+        remote(sku_ref, raw.at[there], sku_sent.at[step], sku_landed.at[there], there, col).wait_recv()
+        remote(
+            probe_raw.at[there], probe_raw.at[there], probe_sent.at[step], probe_landed.at[there], there, col
+        ).wait_recv()
+
+    for there in range(ROWS):
+        folded = probe_raw[there].astype(jnp.float32)
+        for piece in range(ROWS):
+            probe_wide[there * columns : (there + 1) * columns, piece * fold : (piece + 1) * fold] = folded[
+                piece * columns : (piece + 1) * columns
+            ]
+    for side in range(2):
+        lanes = slice(side * half, (side + 1) * half)
+        wide = raw[:, :, lanes].reshape(factors, half).astype(jnp.float32)
+        scale = lax.rsqrt(jnp.sum(wide * wide, axis=0, keepdims=True) + 1e-06)
+        unit = (wide * scale).astype(jnp.bfloat16)
+        full[0, side, 0:factors, :] = unit
+        full[0, side, factors:, :] = probe_wide[:, lanes].astype(jnp.bfloat16)
+        units[0, lanes, :] = unit.T
+
+    pair = remote(full.at[0, core], full.at[1, core], pair_sent, pair_landed, row, mate)
+    send(pair)
+    relay = remote(full.at[1, core], full.at[1, core], twin_sent, twin_landed, twin, col)
+
+    def image_block(which, place):
+        strip = strips[place]
+        total = jnp.zeros((block, strip.shape[1]), jnp.float32)
+        for first in range(0, skus, CHUNK):
+            corr = jnp.dot(units[which, first : first + CHUNK, :], strip, preferred_element_type=jnp.float32)
+            affinity = jnp.exp(corr).astype(jnp.bfloat16)
+            side, lane = first // half, first % half
+            total = total + jnp.dot(
+                full[which, side, factors:, lane : lane + CHUNK], affinity, preferred_element_type=jnp.float32
+            )
+        return total
+
+    def own_half(step, carry):
+        place = other(z, step)
+
+        @pl.when(step > 0)
+        def _():
+            remote(
+                strips.at[place], strips.at[place], strip_sent.at[step], strip_landed.at[place], row, line_col(place)
+            ).wait_recv()
+
+        partial[place] = image_block(0, place)
+
+        @pl.when(step == 2)
+        def _():
+            pair.wait_recv()
+            relay.start()
+
+        return carry
+
+    lax.fori_loop(0, LINE, own_half, 0)
+
+    remote(full.at[1, 1 - core], full.at[1, 1 - core], twin_sent, twin_landed, twin, col).wait_recv()
+    for side in range(2):
+        units[1, side * half : (side + 1) * half, :] = full[1, side, 0:factors, :].T
+
+    def mate_half(step, carry):
+        place = other(z, LINE - 1 - step)
+        partial[place] += image_block(1, place)
+
+        @pl.when(step < LINE - 1)
+        def _():
+            remote(
+                partial.at[place], arrived.at[z], image_sent.at[step], image_landed.at[z], row, line_col(place)
+            ).start()
+
+        return carry
+
+    lax.fori_loop(0, LINE, mate_half, 0)
+
+    image = partial[z]
+    for step in range(1, LINE):
+        place = other(z, step)
+        remote(
+            partial.at[place], arrived.at[place], image_sent.at[step], image_landed.at[place], row, line_col(place)
+        ).wait_recv()
+        image = image + arrived[place]
+
+    local = lax.dot_general(
+        image * weight_ref[...], image, (((1,), (1,)), ((), ())),
+        precision=lax.Precision.HIGHEST, preferred_element_type=jnp.float32,
+    )
+    gram_line[z] = jnp.zeros(gram_line.shape[1:], jnp.float32)
+    gram_line[z, :, 0:block] = local
+    for step in range(1, LINE):
+        there = line_col(other(z, step))
+        send(remote(gram_line.at[z], gram_line.at[z], line_sent.at[step], line_landed.at[z], row, there))
+    for step in range(1, LINE):
+        place = other(z, step)
+        remote(
+            gram_line.at[place], gram_line.at[place], line_sent.at[step], line_landed.at[place], row, line_col(place)
+        ).wait_recv()
+    mine = row * 2 + y
+    gram_group[mine] = (gram_line[0] + gram_line[1]) + (gram_line[2] + gram_line[3])
+    for step in range(1, GROUP):
+        there_row, there_y = other(row, step // 2), (y + step % 2) % 2
+        send(
+            remote(
+                gram_group.at[mine], gram_group.at[mine], group_sent.at[step], group_landed.at[mine],
+                there_row, z * 2 + there_y,
+            )
+        )
+    for step in range(1, GROUP):
+        there_row, there_y = other(row, step // 2), (y + step % 2) % 2
+        slot = there_row * 2 + there_y
+        remote(
+            gram_group.at[slot], gram_group.at[slot], group_sent.at[step], group_landed.at[slot],
+            there_row, z * 2 + there_y,
+        ).wait_recv()
+    gram = gram_group[0]
+    for slot in range(1, GROUP):
+        gram = gram + gram_group[slot]
+
+    rank = lax.broadcasted_iota(jnp.int32, (block, 1), 0)
+    diagonal = jnp.ones((block, 1), jnp.float32)
+    basis = image
+    for k in range(block):
+        pivot = gram[k : k + 1, k : k + 1]
+        diagonal = jnp.where(rank == k, pivot, diagonal)
+        if k < block - 1:
+            factor = jnp.where(rank > k, gram[:, k : k + 1] / pivot, 0.0)
+            gram = gram - factor * gram[k : k + 1, :]
+            basis = basis - factor * basis[k : k + 1, :]
+    out_ref[...] = basis * lax.rsqrt(diagonal)
+
+    for copy in sends:
+        copy.wait_send()
+    relay.wait_send()
+    for step in range(LINE - 1):
+        remote(partial.at[z], arrived.at[z], image_sent.at[step], image_landed.at[z], row, mate).wait_send()
+
+
+def fused_per_device(strip_factors, sku_factors, probe, demand_weight):
+    strip, factors = strip_factors.shape
+    skus, part = sku_factors.shape
+    columns = probe.shape[1]
+    block = ROWS * columns
+    bf16, f32 = jnp.bfloat16, jnp.float32
+    dma = pltpu.SemaphoreType.DMA
+    whole = pl.BlockSpec(memory_space=pltpu.VMEM)
+    return pl.pallas_call(
+        fused,
+        out_shape=jax.ShapeDtypeStruct((block, strip), f32),
+        in_specs=[whole] * 4,
+        out_specs=whole,
+        scratch_shapes=[
+            pltpu.VMEM((ROWS, part, skus), bf16),
+            pltpu.VMEM((ROWS, block, skus // ROWS), bf16),
+            pltpu.VMEM((block, skus // ROWS), f32),
+            pltpu.VMEM((block, skus), f32),
+            pltpu.VMEM((2, 2, factors + block, skus // 2), bf16),
+            pltpu.VMEM((2, skus, factors), bf16),
+            pltpu.VMEM((LINE, factors, strip), bf16),
+            pltpu.VMEM((LINE, block, strip), f32),
+            pltpu.VMEM((LINE, block, strip), f32),
+            pltpu.VMEM((LINE, block, 128), f32),
+            pltpu.VMEM((GROUP, block, 128), f32),
+        ]
+        + [dma((ROWS,))] * 4 + [dma((LINE,))] * 2 + [dma] * 4 + [dma((LINE,))] * 4 + [dma((GROUP,))] * 2,
+        compiler_params=pltpu.CompilerParams(
+            collective_id=0, has_side_effects=True, vmem_limit_bytes=48 * 1024 * 1024
+        ),
+        cost_estimate=pl.CostEstimate(
+            flops=2 * LINE * strip * 2 * skus * (factors + block),
+            bytes_accessed=2 * (strip * factors + skus * part + skus * columns) + 4 * block * strip,
+            transcendentals=LINE * strip * 2 * skus,
+        ),
+    )(strip_factors.T, sku_factors.T, probe.T, demand_weight)
+
+
+def fits(mesh):
+    return mesh.shape["row"] == ROWS and mesh.shape["col"] == 2 * LINE
+
+
 def solution(mesh):
     placed = (P(("row", "col"), None), P("col", "row"), P("col", "row"), P(None, ("row", "col")))
+    plan = fused_per_device if fits(mesh) else per_device
     return jax.shard_map(
-        per_device, mesh=mesh, in_specs=placed, out_specs=P(None, ("row", "col")), check_vma=False
+        plan, mesh=mesh, in_specs=placed, out_specs=P(None, ("row", "col")), check_vma=False
     )

time: 180 us -> 37.1 us (0.21)
  blocking collectives: 85.1 us -> 0 us
  waiting for transfers between devices: 62.1 us -> 0 us
  Pallas kernels: 0 us -> 33.1 us
  between operations: 13.4 us -> 0.01 us
  matrix products: 12.7 us -> 0 us
  other arithmetic: 5.87 us -> 0 us
  local copies, waits for them, and re-layouts: 0.09 us -> 3.69 us
    reduce_scatter x1 -> x0, waiting for transfers between devices: 62.1 us -> none  [per_device(): image = lax.psum_scatter(total, 'col', scatter_dimension=1, tiled=True)]
    all_gather x3 -> x0, blocking collectives: 44.9 us -> none  [the longest x1 32 us: per_device(): piece = lax.all_gather(strip_unit, 'col', axis=0, tiled=True)]
    psum x1 -> x0, blocking collectives: 40.2 us -> none  [per_device(): gram = lax.psum(local_gram, ('row', 'col'))]
    pallas_call x0 -> x1, Pallas kernels: none -> 33.1 us  [fused_per_device(): pl.pallas_call(fused, out_shape=jax.ShapeDtypeStruct((block, strip), f32)...]
    dot_general x5 -> x0, matrix products: 11.1 us -> none  [the longest x4 10.1 us: per_device(): lax.dot_general(block_probe, affinity, (((0,), (1,)), ((), ())), preferre...]
    another operation x5 -> x0, other arithmetic: 4.01 us -> none  [the longest x3 2.13 us: per_device(): lower = jnp.linalg.cholesky(gram)]
    unnamed x3 -> x9, local copies, waits for them, and re-layouts: 0.02 us -> 3.69 us
  transfers between devices with their start and end apart: 1 -> 0, of which waited for: 1 -> 0; matrix products, arithmetic and copies ran while one was open for 0% -> 0% of each run, Pallas kernels for 0% -> 0%
where the time goes in v1:
time: 37.1 us; the launch traced here: 36.9 us
  Pallas kernels  33.1 us (89%)
  local copies, waits for them, and re-layouts  3.69 us (10%)
    pallas_call x1, Pallas kernels, fused_per_device(): pl.pallas_call(fused, out_shape=jax.ShapeDtypeStruct((block, strip), f32)...  33.1 us
    unnamed x9, local copies, waits for them, and re-layouts  3.69 us

profile of v1, /device:TPU:0, one launch (start us, length us, event | category | flops | bytes accessed | tf_op | source)
XLA Modules:
  0.0 36.9 jit_solution(17662450818374603238)
XLA Ops:
  0.0 0.0 copy-start.3
  0.0 0.7 %copy-done.3 = f32[1,512]{1,0:T(1,128)S(1)} copy-done((f32[1,512]{1,0:T(1,128)S(1)}, f32[1,512]{1,0:T(1,128)}, u32[]{:S(2)}) %copy-start.3) | copy-done | bytes 2072
  0.7 0.0 copy-start
  0.7 0.8 %copy-done = bf16[512,64]{0,1:T(8,128)(2,1)S(1)} copy-done((bf16[512,64]{0,1:T(8,128)(2,1)S(1)}, bf16[512,64]{0,1:T(8,128)(2,1)}, u32[]{:S(2)}) %copy-start) | copy-done | bytes 65560
  1.5 0.0 copy-start.1
  1.5 0.8 %copy-done.1 = bf16[2048,16]{0,1:T(8,128)(2,1)S(1)} copy-done((bf16[2048,16]{0,1:T(8,128)(2,1)S(1)}, bf16[2048,16]{0,1:T(8,128)(2,1)}, u32[]{:S(2)}) %copy-start.1) | copy-done | bytes 65560
  2.4 0.0 copy-start.2
  2.4 0.7 %copy-done.2 = bf16[2048,4]{0,1:T(4,128)(2,1)S(1)} copy-done((bf16[2048,4]{0,1:T(4,128)(2,1)S(1)}, bf16[2048,4]{0,1:T(4,128)(2,1)}, u32[]{:S(2)}) %copy-start.2) | copy-done | bytes 16408
  3.1 33.1 %shard_map.46 = f32[16,512]{1,0:T(8,128)S(1)} custom-call(bf16[64,512]{1,0:T(8,128)(2,1)S(1)} %bitcast.3, bf16[16,2048]{1,0:T(8,128)(2,1)S(1)} %bitcast.4, bf16[4,2048]{1,0:T(4,128)(2,1)S(1)} %bitcast.5, f32[1,512]{1,0:T(1,128)S(1)} %copy-done.3), custom_call_target="tpu_custom_call" | custom-call | flops 1342177280 | bytes 180224 | tf_op jit(solution)/shard_map/pallas_call | solution.py:268
  36.2 0.6 %copy.6 = f32[16,512]{1,0:T(8,128)} copy(f32[16,512]{1,0:T(8,128)S(1)} %shard_map.46) | data formatting | bytes 65536
Async XLA Ops:
  0.0 0.7 %copy-start.3 = (f32[1,512]{1,0:T(1,128)S(1)}, f32[1,512]{1,0:T(1,128)}, u32[]{:S(2)}) copy-start(f32[1,512]{1,0:T(1,128)} %weight_ref.1) | copy-start | bytes 6148
  0.7 0.8 %copy-start = (bf16[512,64]{0,1:T(8,128)(2,1)S(1)}, bf16[512,64]{0,1:T(8,128)(2,1)}, u32[]{:S(2)}) copy-start(bf16[512,64]{0,1:T(8,128)(2,1)} %param.4) | copy-start | bytes 196612
  1.5 0.8 %copy-start.1 = (bf16[2048,16]{0,1:T(8,128)(2,1)S(1)}, bf16[2048,16]{0,1:T(8,128)(2,1)}, u32[]{:S(2)}) copy-start(bf16[2048,16]{0,1:T(8,128)(2,1)} %param.5) | copy-start | bytes 196612
  2.4 0.7 %copy-start.2 = (bf16[2048,4]{0,1:T(4,128)(2,1)S(1)}, bf16[2048,4]{0,1:T(4,128)(2,1)}, u32[]{:S(2)}) copy-start(bf16[2048,4]{0,1:T(4,128)(2,1)} %param.6) | copy-start | bytes 49156

commit v2 on v1

--- a/solution.py
+++ b/solution.py
@@ -8,7 +8,7 @@
 ROWS = 4
 LINE = 4
 GROUP = 2 * ROWS
-CHUNK = 512
+CHUNK = 256
 
 
 def unit_rows(factors):
@@ -64,11 +64,11 @@
 
 
 def fused(
-    strip_ref, sku_ref, probe_ref, weight_ref, out_ref,
-    raw, probe_raw, probe_stage, probe_wide, full, units, strips, partial, arrived, gram_line, gram_group,
+    strip_hbm, sku_ref, probe_hbm, weight_hbm, out_ref,
+    strip_ref, probe_ref, weight_ref, raw, probe_raw, probe_stage, probe_wide, full, units, strips, partial, arrived, gram_line, gram_group,
     sku_sent, sku_landed, probe_sent, probe_landed, strip_sent, strip_landed,
     pair_sent, pair_landed, twin_sent, twin_landed, image_sent, image_landed,
-    line_sent, line_landed, group_sent, group_landed,
+    line_sent, line_landed, group_sent, group_landed, loaded,
 ):
     row, col = lax.axis_index("row"), lax.axis_index("col")
     core = row % 2
@@ -77,6 +77,14 @@
     mate = col + 1 - 2 * y
     part, skus = sku_ref.shape
     columns = probe_ref.shape[0]
+    loads = [
+        pltpu.make_async_copy(source, target, loaded.at[number])
+        for number, (source, target) in enumerate(
+            ((strip_hbm, strip_ref), (probe_hbm, probe_ref), (weight_hbm, weight_ref), (sku_ref, raw.at[row]))
+        )
+    ]
+    for load in loads:
+        load.start()
     factors = ROWS * part
     block = ROWS * columns
     half = skus // 2
@@ -93,12 +101,13 @@
     for step in range(ROWS):
         pl.semaphore_signal(barrier, inc=1, device_id=(other(row, step), mate), device_id_type=pl.DeviceIdType.MESH)
 
-    raw[row] = sku_ref[...]
+    loads[1].wait()
     for piece in range(ROWS):
         probe_stage[piece * columns : (piece + 1) * columns, :] = probe_ref[
             :, piece * fold : (piece + 1) * fold
         ].astype(jnp.float32)
     probe_raw[row] = probe_stage[...].astype(jnp.bfloat16)
+    loads[0].wait()
     wide = strip_ref[...].astype(jnp.float32)
     scale = lax.rsqrt(jnp.sum(wide * wide, axis=0, keepdims=True) + 1e-06)
     strips[z] = (wide * scale).astype(jnp.bfloat16)
@@ -126,6 +135,7 @@
             probe_raw.at[there], probe_raw.at[there], probe_sent.at[step], probe_landed.at[there], there, col
         ).wait_recv()
 
+    loads[3].wait()
     for there in range(ROWS):
         folded = probe_raw[there].astype(jnp.float32)
         for piece in range(ROWS):
@@ -146,16 +156,19 @@
     relay = remote(full.at[1, core], full.at[1, core], twin_sent, twin_landed, twin, col)
 
     def image_block(which, place):
-        strip = strips[place]
-        total = jnp.zeros((block, strip.shape[1]), jnp.float32)
-        for first in range(0, skus, CHUNK):
-            corr = jnp.dot(units[which, first : first + CHUNK, :], strip, preferred_element_type=jnp.float32)
-            affinity = jnp.exp(corr).astype(jnp.bfloat16)
-            side, lane = first // half, first % half
-            total = total + jnp.dot(
-                full[which, side, factors:, lane : lane + CHUNK], affinity, preferred_element_type=jnp.float32
-            )
-        return total
+        totals = []
+        for left in range(0, strips.shape[2], CHUNK):
+            strip = strips[place, :, left : left + CHUNK]
+            total = jnp.zeros((block, CHUNK), jnp.float32)
+            for first in range(0, skus, CHUNK):
+                corr = jnp.dot(units[which, first : first + CHUNK, :], strip, preferred_element_type=jnp.float32)
+                affinity = jnp.exp(corr).astype(jnp.bfloat16)
+                side, lane = first // half, first % half
+                total = total + jnp.dot(
+                    full[which, side, factors:, lane : lane + CHUNK], affinity, preferred_element_type=jnp.float32
+                )
+            totals.append(total)
+        return jnp.concatenate(totals, axis=1)
 
     def own_half(step, carry):
         place = other(z, step)
@@ -203,6 +216,7 @@
         ).wait_recv()
         image = image + arrived[place]
 
+    loads[2].wait()
     local = lax.dot_general(
         image * weight_ref[...], image, (((1,), (1,)), ((), ())),
         precision=lax.Precision.HIGHEST, preferred_element_type=jnp.float32,
@@ -265,12 +279,16 @@
     bf16, f32 = jnp.bfloat16, jnp.float32
     dma = pltpu.SemaphoreType.DMA
     whole = pl.BlockSpec(memory_space=pltpu.VMEM)
+    far = pl.BlockSpec(memory_space=pltpu.HBM)
     return pl.pallas_call(
         fused,
         out_shape=jax.ShapeDtypeStruct((block, strip), f32),
-        in_specs=[whole] * 4,
+        in_specs=[far] * 4,
         out_specs=whole,
         scratch_shapes=[
+            pltpu.VMEM((factors, strip), bf16),
+            pltpu.VMEM((columns, skus), bf16),
+            pltpu.VMEM((1, strip), f32),
             pltpu.VMEM((ROWS, part, skus), bf16),
             pltpu.VMEM((ROWS, block, skus // ROWS), bf16),
             pltpu.VMEM((block, skus // ROWS), f32),
@@ -283,9 +301,9 @@
             pltpu.VMEM((LINE, block, 128), f32),
             pltpu.VMEM((GROUP, block, 128), f32),
         ]
-        + [dma((ROWS,))] * 4 + [dma((LINE,))] * 2 + [dma] * 4 + [dma((LINE,))] * 4 + [dma((GROUP,))] * 2,
+        + [dma((ROWS,))] * 4 + [dma((LINE,))] * 2 + [dma] * 4 + [dma((LINE,))] * 4 + [dma((GROUP,))] * 2 + [dma((4,))],
         compiler_params=pltpu.CompilerParams(
-            collective_id=0, has_side_effects=True, vmem_limit_bytes=48 * 1024 * 1024
+            collective_id=0, has_side_effects=True, vmem_limit_bytes=60 * 1024 * 1024
         ),
         cost_estimate=pl.CostEstimate(
             flops=2 * LINE * strip * 2 * skus * (factors + block),

time: 37.1 us -> 37.7 us (1.016)
  Pallas kernels: 33.1 us -> 36.1 us
  local copies, waits for them, and re-layouts: 3.69 us -> 1.38 us
    pallas_call x1, Pallas kernels: 33.1 us -> 36.1 us  [fused_per_device(): pl.pallas_call(fused, out_shape=jax.ShapeDtypeStruct((block, strip), f32)...]
    unnamed x9 -> x1, local copies, waits for them, and re-layouts: 3.69 us -> 1.38 us
where the time goes in v2:
time: 37.7 us; the launch traced here: 37.5 us
  Pallas kernels  36.1 us (96%)
  local copies, waits for them, and re-layouts  1.38 us (4%)
    pallas_call x1, Pallas kernels, fused_per_device(): pl.pallas_call(fused, out_shape=jax.ShapeDtypeStruct((block, strip), f32)...  36.1 us
    unnamed x1, local copies, waits for them, and re-layouts  1.38 us

profile of v2, /device:TPU:0, one launch (start us, length us, event | category | flops | bytes accessed | tf_op | source)
XLA Modules:
  0.0 37.5 jit_solution(15790148507614187188)
XLA Ops:
  0.0 36.1 %shard_map.46 = f32[16,512]{1,0:T(8,128)} custom-call(bf16[64,512]{1,0:T(8,128)(2,1)} %bitcast.3, bf16[16,2048]{1,0:T(8,128)(2,1)} %bitcast.4, bf16[4,2048]{1,0:T(4,128)(2,1)} %bitcast.5, f32[1,512]{1,0:T(1,128)} %weight_hbm.1), custom_call_target="tpu_custom_call" | custom-call | flops 1342177280 | bytes 180224 | tf_op jit(solution)/shard_map/pallas_call | solution.py:283
  36.1 1.4 %copy.6 = f32[16,512]{1,0:T(8,128)} copy(f32[16,512]{1,0:T(8,128)} %shard_map.46) | data formatting | bytes 65536

commit v3 on v2

--- a/solution.py
+++ b/solution.py
@@ -8,7 +8,7 @@
 ROWS = 4
 LINE = 4
 GROUP = 2 * ROWS
-CHUNK = 256
+CHUNK = 512
 
 
 def unit_rows(factors):
@@ -252,17 +252,22 @@
     for slot in range(1, GROUP):
         gram = gram + gram_group[slot]
 
-    rank = lax.broadcasted_iota(jnp.int32, (block, 1), 0)
-    diagonal = jnp.ones((block, 1), jnp.float32)
-    basis = image
+    lanes = 128
+    rank = lax.broadcasted_iota(jnp.int32, (block, lanes), 0)
+    pivots = [jnp.broadcast_to(gram[:, k : k + 1], (block, lanes)) for k in range(block)]
+    pieces = [image[:, left : left + lanes] for left in range(0, image.shape[1], lanes)]
+    diagonal = jnp.ones((block, lanes), jnp.float32)
     for k in range(block):
-        pivot = gram[k : k + 1, k : k + 1]
+        pivot = pivots[k][k : k + 1, :]
         diagonal = jnp.where(rank == k, pivot, diagonal)
         if k < block - 1:
-            factor = jnp.where(rank > k, gram[:, k : k + 1] / pivot, 0.0)
-            gram = gram - factor * gram[k : k + 1, :]
-            basis = basis - factor * basis[k : k + 1, :]
-    out_ref[...] = basis * lax.rsqrt(diagonal)
+            factor = jnp.where(rank > k, pivots[k] * (1.0 / pivot), 0.0)
+            for later in range(k + 1, block):
+                pivots[later] = pivots[later] - factor * pivots[later][k : k + 1, :]
+            pieces = [piece - factor * piece[k : k + 1, :] for piece in pieces]
+    root = lax.rsqrt(diagonal)
+    for number, piece in enumerate(pieces):
+        out_ref[:, number * lanes : (number + 1) * lanes] = piece * root
 
     for copy in sends:
         copy.wait_send()

time: 37.7 us -> 34.6 us (0.918)
  Pallas kernels: 36.1 us -> 33 us
    pallas_call x1, Pallas kernels: 36.1 us -> 33 us  [fused_per_device(): pl.pallas_call(fused, out_shape=jax.ShapeDtypeStruct((block, strip), f32)...]
where the time goes in v3:
time: 34.6 us; the launch traced here: 34.4 us
  Pallas kernels  33 us (95%)
  local copies, waits for them, and re-layouts  1.38 us (4%)
    pallas_call x1, Pallas kernels, fused_per_device(): pl.pallas_call(fused, out_shape=jax.ShapeDtypeStruct((block, strip), f32)...  33 us
    unnamed x1, local copies, waits for them, and re-layouts  1.38 us

profile of v3, /device:TPU:0, one launch (start us, length us, event | category | flops | bytes accessed | tf_op | source)
XLA Modules:
  0.0 34.4 jit_solution(3262950461218420051)
XLA Ops:
  0.0 33.0 %shard_map.46 = f32[16,512]{1,0:T(8,128)} custom-call(bf16[64,512]{1,0:T(8,128)(2,1)} %bitcast.3, bf16[16,2048]{1,0:T(8,128)(2,1)} %bitcast.4, bf16[4,2048]{1,0:T(4,128)(2,1)} %bitcast.5, f32[1,512]{1,0:T(1,128)} %weight_hbm.1), custom_call_target="tpu_custom_call" | custom-call | flops 1342177280 | bytes 180224 | tf_op jit(solution)/shard_map/pallas_call | solution.py:288
  33.0 1.4 %copy.6 = f32[16,512]{1,0:T(8,128)} copy(f32[16,512]{1,0:T(8,128)} %shard_map.46) | data formatting | bytes 65536

commit v4 on v3

--- a/solution.py
+++ b/solution.py
@@ -120,83 +120,102 @@
         copy.start()
         sends.append(copy)
 
+    def sku_copy(side, step, there, slot):
+        lanes = slice(side * half, (side + 1) * half)
+        return remote(
+            sku_ref.at[:, lanes], raw.at[slot, :, lanes], sku_sent.at[side, step], sku_landed.at[side, slot], there, col
+        )
+
+    for step in (2, 3, 1):
+        send(sku_copy(0, step, other(row, step), row))
     for step in (2, 3, 1):
         there = other(row, step)
-        send(remote(sku_ref, raw.at[row], sku_sent.at[step], sku_landed.at[row], there, col))
         send(remote(probe_raw.at[row], probe_raw.at[row], probe_sent.at[step], probe_landed.at[row], there, col))
+    for step in (2, 3, 1):
+        send(sku_copy(1, step, other(row, step), row))
     for step in range(1, LINE):
         there = line_col(other(z, step))
         send(remote(strips.at[z], strips.at[z], strip_sent.at[step], strip_landed.at[z], row, there))
 
+    loads[3].wait()
     for step in range(1, ROWS):
         there = other(row, step)
-        remote(sku_ref, raw.at[there], sku_sent.at[step], sku_landed.at[there], there, col).wait_recv()
         remote(
             probe_raw.at[there], probe_raw.at[there], probe_sent.at[step], probe_landed.at[there], there, col
         ).wait_recv()
-
-    loads[3].wait()
     for there in range(ROWS):
         folded = probe_raw[there].astype(jnp.float32)
         for piece in range(ROWS):
             probe_wide[there * columns : (there + 1) * columns, piece * fold : (piece + 1) * fold] = folded[
                 piece * columns : (piece + 1) * columns
             ]
+
+    pair = remote(full.at[0, core], full.at[1, core], pair_sent, pair_landed, row, mate)
+    relay = remote(full.at[1, core], full.at[1, core], twin_sent, twin_landed, twin, col)
+
+    def image_block(which, side, place):
+        strip = strips[place]
+        total = jnp.zeros((block, strip.shape[1]), jnp.float32)
+        for first in range(0, half, CHUNK):
+            corr = jnp.dot(units[which, side, first : first + CHUNK, :], strip, preferred_element_type=jnp.float32)
+            affinity = jnp.exp(corr).astype(jnp.bfloat16)
+            total = total + jnp.dot(
+                full[which, side, factors:, first : first + CHUNK], affinity, preferred_element_type=jnp.float32
+            )
+        return total
+
     for side in range(2):
+        for step in range(1, ROWS):
+            there = other(row, step)
+            sku_copy(side, step, there, there).wait_recv()
         lanes = slice(side * half, (side + 1) * half)
         wide = raw[:, :, lanes].reshape(factors, half).astype(jnp.float32)
         scale = lax.rsqrt(jnp.sum(wide * wide, axis=0, keepdims=True) + 1e-06)
         unit = (wide * scale).astype(jnp.bfloat16)
         full[0, side, 0:factors, :] = unit
         full[0, side, factors:, :] = probe_wide[:, lanes].astype(jnp.bfloat16)
-        units[0, lanes, :] = unit.T
-
-    pair = remote(full.at[0, core], full.at[1, core], pair_sent, pair_landed, row, mate)
-    send(pair)
-    relay = remote(full.at[1, core], full.at[1, core], twin_sent, twin_landed, twin, col)
-
-    def image_block(which, place):
-        totals = []
-        for left in range(0, strips.shape[2], CHUNK):
-            strip = strips[place, :, left : left + CHUNK]
-            total = jnp.zeros((block, CHUNK), jnp.float32)
-            for first in range(0, skus, CHUNK):
-                corr = jnp.dot(units[which, first : first + CHUNK, :], strip, preferred_element_type=jnp.float32)
-                affinity = jnp.exp(corr).astype(jnp.bfloat16)
-                side, lane = first // half, first % half
-                total = total + jnp.dot(
-                    full[which, side, factors:, lane : lane + CHUNK], affinity, preferred_element_type=jnp.float32
-                )
-            totals.append(total)
-        return jnp.concatenate(totals, axis=1)
-
-    def own_half(step, carry):
-        place = other(z, step)
-
-        @pl.when(step > 0)
+        units[0, side] = unit.T
+
+        @pl.when(core == side)
         def _():
-            remote(
-                strips.at[place], strips.at[place], strip_sent.at[step], strip_landed.at[place], row, line_col(place)
-            ).wait_recv()
-
-        partial[place] = image_block(0, place)
-
-        @pl.when(step == 2)
-        def _():
-            pair.wait_recv()
-            relay.start()
-
+            pair.start()
+
+        def own_side(step, carry):
+            place = other(z, step)
+            if side == 0:
+
+                @pl.when(step > 0)
+                def _():
+                    remote(
+                        strips.at[place], strips.at[place], strip_sent.at[step], strip_landed.at[place],
+                        row, line_col(place),
+                    ).wait_recv()
+
+                partial[place] = image_block(0, side, place)
+            else:
+                partial[place] += image_block(0, side, place)
+            return carry
+
+        lax.fori_loop(0, LINE, own_side, 0)
+
+    pair.wait_recv()
+    relay.start()
+    units[1, core] = full[1, core, 0:factors, :].T
+
+    def mate_first(step, carry):
+        place = other(z, LINE - 1 - step)
+        partial[place] += image_block(1, core, place)
         return carry
 
-    lax.fori_loop(0, LINE, own_half, 0)
-
-    remote(full.at[1, 1 - core], full.at[1, 1 - core], twin_sent, twin_landed, twin, col).wait_recv()
-    for side in range(2):
-        units[1, side * half : (side + 1) * half, :] = full[1, side, 0:factors, :].T
-
-    def mate_half(step, carry):
+    lax.fori_loop(0, LINE, mate_first, 0)
+
+    last = 1 - core
+    remote(full.at[1, last], full.at[1, last], twin_sent, twin_landed, twin, col).wait_recv()
+    units[1, last] = full[1, last, 0:factors, :].T
+
+    def mate_last(step, carry):
         place = other(z, LINE - 1 - step)
-        partial[place] += image_block(1, place)
+        partial[place] += image_block(1, last, place)
 
         @pl.when(step < LINE - 1)
         def _():
@@ -206,7 +225,7 @@
 
         return carry
 
-    lax.fori_loop(0, LINE, mate_half, 0)
+    lax.fori_loop(0, LINE, mate_last, 0)
 
     image = partial[z]
     for step in range(1, LINE):
@@ -271,6 +290,7 @@
 
     for copy in sends:
         copy.wait_send()
+    pair.wait_send()
     relay.wait_send()
     for step in range(LINE - 1):
         remote(partial.at[z], arrived.at[z], image_sent.at[step], image_landed.at[z], row, mate).wait_send()
@@ -287,7 +307,7 @@
     far = pl.BlockSpec(memory_space=pltpu.HBM)
     return pl.pallas_call(
         fused,
-        out_shape=jax.ShapeDtypeStruct((block, strip), f32),
+        out_shape=pltpu.VMEM((block, strip), f32),
         in_specs=[far] * 4,
         out_specs=whole,
         scratch_shapes=[
@@ -299,14 +319,14 @@
             pltpu.VMEM((block, skus // ROWS), f32),
             pltpu.VMEM((block, skus), f32),
             pltpu.VMEM((2, 2, factors + block, skus // 2), bf16),
-            pltpu.VMEM((2, skus, factors), bf16),
+            pltpu.VMEM((2, 2, skus // 2, factors), bf16),
             pltpu.VMEM((LINE, factors, strip), bf16),
             pltpu.VMEM((LINE, block, strip), f32),
             pltpu.VMEM((LINE, block, strip), f32),
             pltpu.VMEM((LINE, block, 128), f32),
             pltpu.VMEM((GROUP, block, 128), f32),
         ]
-        + [dma((ROWS,))] * 4 + [dma((LINE,))] * 2 + [dma] * 4 + [dma((LINE,))] * 4 + [dma((GROUP,))] * 2 + [dma((4,))],
+        + [dma((2, ROWS))] * 2 + [dma((ROWS,))] * 2 + [dma((LINE,))] * 2 + [dma] * 4 + [dma((LINE,))] * 4 + [dma((GROUP,))] * 2 + [dma((4,))],
         compiler_params=pltpu.CompilerParams(
             collective_id=0, has_side_effects=True, vmem_limit_bytes=60 * 1024 * 1024
         ),

time: 34.6 us -> 33 us (0.954)
  Pallas kernels: 33 us -> 32.2 us
  local copies, waits for them, and re-layouts: 1.38 us -> 0.62 us
    pallas_call x1, Pallas kernels: 33 us -> 32.2 us  [fused_per_device(): pl.pallas_call(fused, out_shape=pltpu.VMEM((block, strip), f32), in_specs...]
    unnamed x1, local copies, waits for them, and re-layouts: 1.38 us -> 0.62 us
where the time goes in v4:
time: 33 us; the launch traced here: 32.8 us
  Pallas kernels  32.2 us (98%)
  local copies, waits for them, and re-layouts  0.62 us (2%)
    pallas_call x1, Pallas kernels, fused_per_device(): pl.pallas_call(fused, out_shape=pltpu.VMEM((block, strip), f32), in_specs...  32.2 us

profile of v4, /device:TPU:0, one launch (start us, length us, event | category | flops | bytes accessed | tf_op | source)
XLA Modules:
  0.0 32.8 jit_solution(15561792100218089522)
XLA Ops:
  0.0 32.2 %shard_map.46 = f32[16,512]{1,0:T(8,128)S(1)} custom-call(bf16[64,512]{1,0:T(8,128)(2,1)} %bitcast.3, bf16[16,2048]{1,0:T(8,128)(2,1)} %bitcast.4, bf16[4,2048]{1,0:T(4,128)(2,1)} %bitcast.5, f32[1,512]{1,0:T(1,128)} %weight_hbm.1), custom_call_target="tpu_custom_call" | custom-call | flops 1342177280 | bytes 180224 | tf_op jit(solution)/shard_map/pallas_call | solution.py:308
  32.2 0.6 %copy.6 = f32[16,512]{1,0:T(8,128)} copy(f32[16,512]{1,0:T(8,128)S(1)} %shard_map.46) | data formatting | bytes 65536

commit v5 on v4

--- a/solution.py
+++ b/solution.py
@@ -8,7 +8,8 @@
 ROWS = 4
 LINE = 4
 GROUP = 2 * ROWS
-CHUNK = 512
+CHUNK = 1024
+LOG2_E = 1.4426950408889634
 
 
 def unit_rows(factors):
@@ -158,7 +159,7 @@
         total = jnp.zeros((block, strip.shape[1]), jnp.float32)
         for first in range(0, half, CHUNK):
             corr = jnp.dot(units[which, side, first : first + CHUNK, :], strip, preferred_element_type=jnp.float32)
-            affinity = jnp.exp(corr).astype(jnp.bfloat16)
+            affinity = jnp.exp2(corr * LOG2_E).astype(jnp.bfloat16)
             total = total + jnp.dot(
                 full[which, side, factors:, first : first + CHUNK], affinity, preferred_element_type=jnp.float32
             )

time: 33 us -> 32.4 us (0.982)
  Pallas kernels: 32.2 us -> 31.6 us
    pallas_call x1, Pallas kernels: 32.2 us -> 31.6 us  [fused_per_device(): pl.pallas_call(fused, out_shape=pltpu.VMEM((block, strip), f32), in_specs...]
where the time goes in v5:
time: 32.4 us; the launch traced here: 32.2 us
  Pallas kernels  31.6 us (98%)
  local copies, waits for them, and re-layouts  0.62 us (2%)
    pallas_call x1, Pallas kernels, fused_per_device(): pl.pallas_call(fused, out_shape=pltpu.VMEM((block, strip), f32), in_specs...  31.6 us

profile of v5, /device:TPU:0, one launch (start us, length us, event | category | flops | bytes accessed | tf_op | source)
XLA Modules:
  0.0 32.2 jit_solution(14367615447880477072)
XLA Ops:
  0.0 31.6 %shard_map.46 = f32[16,512]{1,0:T(8,128)S(1)} custom-call(bf16[64,512]{1,0:T(8,128)(2,1)} %bitcast.3, bf16[16,2048]{1,0:T(8,128)(2,1)} %bitcast.4, bf16[4,2048]{1,0:T(4,128)(2,1)} %bitcast.5, f32[1,512]{1,0:T(1,128)} %weight_hbm.1), custom_call_target="tpu_custom_call" | custom-call | flops 1342177280 | bytes 180224 | tf_op jit(solution)/shard_map/pallas_call | solution.py:309
  31.6 0.6 %copy.6 = f32[16,512]{1,0:T(8,128)} copy(f32[16,512]{1,0:T(8,128)S(1)} %shard_map.46) | data formatting | bytes 65536

commit v6 on v5

--- a/solution.py
+++ b/solution.py
@@ -102,38 +102,37 @@
     for step in range(ROWS):
         pl.semaphore_signal(barrier, inc=1, device_id=(other(row, step), mate), device_id_type=pl.DeviceIdType.MESH)
 
+    sends = []
+
+    def send(copy):
+        copy.start()
+        sends.append(copy)
+
+    def sku_copy(side, step, there, slot):
+        lanes = slice(side * half, (side + 1) * half)
+        return remote(
+            sku_ref.at[:, lanes], raw.at[slot, :, lanes], sku_sent.at[side, step], sku_landed.at[side, slot], there, col
+        )
+
+    pl.semaphore_wait(barrier, 2 * ROWS + LINE - 2)
+
+    for step in (2, 3, 1):
+        send(sku_copy(0, step, other(row, step), row))
     loads[1].wait()
     for piece in range(ROWS):
         probe_stage[piece * columns : (piece + 1) * columns, :] = probe_ref[
             :, piece * fold : (piece + 1) * fold
         ].astype(jnp.float32)
     probe_raw[row] = probe_stage[...].astype(jnp.bfloat16)
-    loads[0].wait()
-    wide = strip_ref[...].astype(jnp.float32)
-    scale = lax.rsqrt(jnp.sum(wide * wide, axis=0, keepdims=True) + 1e-06)
-    strips[z] = (wide * scale).astype(jnp.bfloat16)
-
-    pl.semaphore_wait(barrier, 2 * ROWS + LINE - 2)
-
-    sends = []
-
-    def send(copy):
-        copy.start()
-        sends.append(copy)
-
-    def sku_copy(side, step, there, slot):
-        lanes = slice(side * half, (side + 1) * half)
-        return remote(
-            sku_ref.at[:, lanes], raw.at[slot, :, lanes], sku_sent.at[side, step], sku_landed.at[side, slot], there, col
-        )
-
-    for step in (2, 3, 1):
-        send(sku_copy(0, step, other(row, step), row))
     for step in (2, 3, 1):
         there = other(row, step)
         send(remote(probe_raw.at[row], probe_raw.at[row], probe_sent.at[step], probe_landed.at[row], there, col))
     for step in (2, 3, 1):
         send(sku_copy(1, step, other(row, step), row))
+    loads[0].wait()
+    wide = strip_ref[...].astype(jnp.float32)
+    scale = lax.rsqrt(jnp.sum(wide * wide, axis=0, keepdims=True) + 1e-06)
+    strips[z] = (wide * scale).astype(jnp.bfloat16)
     for step in range(1, LINE):
         there = line_col(other(z, step))
         send(remote(strips.at[z], strips.at[z], strip_sent.at[step], strip_landed.at[z], row, there))
@@ -197,7 +196,7 @@
                 partial[place] += image_block(0, side, place)
             return carry
 
-        lax.fori_loop(0, LINE, own_side, 0)
+        lax.fori_loop(side, LINE, own_side, 0)
 
     pair.wait_recv()
     relay.start()
@@ -208,7 +207,7 @@
         partial[place] += image_block(1, core, place)
         return carry
 
-    lax.fori_loop(0, LINE, mate_first, 0)
+    lax.fori_loop(0, LINE - 1, mate_first, 0)
 
     last = 1 - core
     remote(full.at[1, last], full.at[1, last], twin_sent, twin_landed, twin, col).wait_recv()
@@ -218,17 +217,14 @@
         place = other(z, LINE - 1 - step)
         partial[place] += image_block(1, last, place)
 
-        @pl.when(step < LINE - 1)
-        def _():
-            remote(
-                partial.at[place], arrived.at[z], image_sent.at[step], image_landed.at[z], row, line_col(place)
-            ).start()
-
+        remote(
+            partial.at[place], arrived.at[z], image_sent.at[step], image_landed.at[z], row, line_col(place)
+        ).start()
         return carry
 
-    lax.fori_loop(0, LINE, mate_last, 0)
-
-    image = partial[z]
+    lax.fori_loop(0, LINE - 1, mate_last, 0)
+
+    image = partial[z] + image_block(0, 1, z) + image_block(1, 0, z) + image_block(1, 1, z)
     for step in range(1, LINE):
         place = other(z, step)
         remote(

time: 32.4 us -> 31.6 us (0.975)
  Pallas kernels: 31.6 us -> 30.8 us
    pallas_call x1, Pallas kernels: 31.6 us -> 30.8 us  [fused_per_device(): pl.pallas_call(fused, out_shape=pltpu.VMEM((block, strip), f32), in_specs...]
where the time goes in v6:
time: 31.6 us; the launch traced here: 31.4 us
  Pallas kernels  30.8 us (97%)
  local copies, waits for them, and re-layouts  0.62 us (2%)
    pallas_call x1, Pallas kernels, fused_per_device(): pl.pallas_call(fused, out_shape=pltpu.VMEM((block, strip), f32), in_specs...  30.8 us

profile of v6, /device:TPU:0, one launch (start us, length us, event | category | flops | bytes accessed | tf_op | source)
XLA Modules:
  0.0 31.4 jit_solution(9405633216691452049)
XLA Ops:
  0.0 30.8 %shard_map.46 = f32[16,512]{1,0:T(8,128)S(1)} custom-call(bf16[64,512]{1,0:T(8,128)(2,1)} %bitcast.3, bf16[16,2048]{1,0:T(8,128)(2,1)} %bitcast.4, bf16[4,2048]{1,0:T(4,128)(2,1)} %bitcast.5, f32[1,512]{1,0:T(1,128)} %weight_hbm.1), custom_call_target="tpu_custom_call" | custom-call | flops 1342177280 | bytes 180224 | tf_op jit(solution)/shard_map/pallas_call | solution.py:305
  30.8 0.6 %copy.6 = f32[16,512]{1,0:T(8,128)} copy(f32[16,512]{1,0:T(8,128)S(1)} %shard_map.46) | data formatting | bytes 65536

commit v7 on v6

--- a/solution.py
+++ b/solution.py
@@ -8,7 +8,7 @@
 ROWS = 4
 LINE = 4
 GROUP = 2 * ROWS
-CHUNK = 1024
+CHUNK = 256
 LOG2_E = 1.4426950408889634
 
 
@@ -153,16 +153,31 @@
     pair = remote(full.at[0, core], full.at[1, core], pair_sent, pair_landed, row, mate)
     relay = remote(full.at[1, core], full.at[1, core], twin_sent, twin_landed, twin, col)
 
+    def image_blocks(tasks):
+        steps = [(number, first) for number in range(len(tasks)) for first in range(0, half, CHUNK)]
+        totals = [jnp.zeros((block, strips.shape[2]), jnp.float32) for _ in tasks]
+        corr = affinity = None
+        for turn in range(len(steps) + 2):
+            corr_next = affinity_next = None
+            if turn < len(steps):
+                number, first = steps[turn]
+                which, side, place = tasks[number]
+                corr_next = jnp.dot(
+                    units[which, side, first : first + CHUNK, :], strips[place], preferred_element_type=jnp.float32
+                )
+            if corr is not None:
+                affinity_next = jnp.exp2(corr * LOG2_E).astype(jnp.bfloat16)
+            if affinity is not None:
+                number, first = steps[turn - 2]
+                which, side, place = tasks[number]
+                totals[number] = totals[number] + jnp.dot(
+                    full[which, side, factors:, first : first + CHUNK], affinity, preferred_element_type=jnp.float32
+                )
+            corr, affinity = corr_next, affinity_next
+        return totals
+
     def image_block(which, side, place):
-        strip = strips[place]
-        total = jnp.zeros((block, strip.shape[1]), jnp.float32)
-        for first in range(0, half, CHUNK):
-            corr = jnp.dot(units[which, side, first : first + CHUNK, :], strip, preferred_element_type=jnp.float32)
-            affinity = jnp.exp2(corr * LOG2_E).astype(jnp.bfloat16)
-            total = total + jnp.dot(
-                full[which, side, factors:, first : first + CHUNK], affinity, preferred_element_type=jnp.float32
-            )
-        return total
+        return image_blocks([(which, side, place)])[0]
 
     for side in range(2):
         for step in range(1, ROWS):
@@ -180,9 +195,10 @@
         def _():
             pair.start()
 
-        def own_side(step, carry):
-            place = other(z, step)
-            if side == 0:
+        if side == 0:
+
+            def own_side(step, carry):
+                place = other(z, step)
 
                 @pl.when(step > 0)
                 def _():
@@ -192,22 +208,20 @@
                     ).wait_recv()
 
                 partial[place] = image_block(0, side, place)
-            else:
-                partial[place] += image_block(0, side, place)
-            return carry
-
-        lax.fori_loop(side, LINE, own_side, 0)
+                return carry
+
+            lax.fori_loop(0, LINE, own_side, 0)
+        else:
+            places = [other(z, step) for step in range(1, LINE)]
+            for place, total in zip(places, image_blocks([(0, side, place) for place in places])):
+                partial[place] += total
 
     pair.wait_recv()
     relay.start()
     units[1, core] = full[1, core, 0:factors, :].T
 
-    def mate_first(step, carry):
-        place = other(z, LINE - 1 - step)
-        partial[place] += image_block(1, core, place)
-        return carry
-
-    lax.fori_loop(0, LINE - 1, mate_first, 0)
+    for place, total in zip(places, image_blocks([(1, core, place) for place in places])):
+        partial[place] += total
 
     last = 1 - core
     remote(full.at[1, last], full.at[1, last], twin_sent, twin_landed, twin, col).wait_recv()
@@ -224,7 +238,7 @@
 
     lax.fori_loop(0, LINE - 1, mate_last, 0)
 
-    image = partial[z] + image_block(0, 1, z) + image_block(1, 0, z) + image_block(1, 1, z)
+    image = partial[z] + sum(image_blocks([(0, 1, z), (1, 0, z), (1, 1, z)]))
     for step in range(1, LINE):
         place = other(z, step)
         remote(

time: 31.6 us -> 31.4 us (level)
  no operation moved by 1% of the time
where the time goes in v7:
time: 31.4 us; the launch traced here: 31.3 us
  Pallas kernels  30.7 us (98%)
  local copies, waits for them, and re-layouts  0.62 us (2%)
    pallas_call x1, Pallas kernels, fused_per_device(): pl.pallas_call(fused, out_shape=pltpu.VMEM((block, strip), f32), in_specs...  30.7 us

profile of v7, /device:TPU:0, one launch (start us, length us, event | category | flops | bytes accessed | tf_op | source)
XLA Modules:
  0.0 31.3 jit_solution(10482714800371321384)
XLA Ops:
  0.0 30.7 %shard_map.46 = f32[16,512]{1,0:T(8,128)S(1)} custom-call(bf16[64,512]{1,0:T(8,128)(2,1)} %bitcast.3, bf16[16,2048]{1,0:T(8,128)(2,1)} %bitcast.4, bf16[4,2048]{1,0:T(4,128)(2,1)} %bitcast.5, f32[1,512]{1,0:T(1,128)} %weight_hbm.1), custom_call_target="tpu_custom_call" | custom-call | flops 1342177280 | bytes 180224 | tf_op jit(solution)/shard_map/pallas_call | solution.py:319
  30.7 0.6 %copy.6 = f32[16,512]{1,0:T(8,128)} copy(f32[16,512]{1,0:T(8,128)S(1)} %shard_map.46) | data formatting | bytes 65536

commit v8 on v7

--- a/solution.py
+++ b/solution.py
@@ -152,6 +152,11 @@
 
     pair = remote(full.at[0, core], full.at[1, core], pair_sent, pair_landed, row, mate)
     relay = remote(full.at[1, core], full.at[1, core], twin_sent, twin_landed, twin, col)
+
+    def strip_wait(place, step):
+        remote(
+            strips.at[place], strips.at[place], strip_sent.at[step], strip_landed.at[place], row, line_col(place)
+        ).wait_recv()
 
     def image_blocks(tasks):
         steps = [(number, first) for number in range(len(tasks)) for first in range(0, half, CHUNK)]
@@ -196,26 +201,23 @@
             pair.start()
 
         if side == 0:
-
-            def own_side(step, carry):
-                place = other(z, step)
-
-                @pl.when(step > 0)
-                def _():
-                    remote(
-                        strips.at[place], strips.at[place], strip_sent.at[step], strip_landed.at[place],
-                        row, line_col(place),
-                    ).wait_recv()
-
-                partial[place] = image_block(0, side, place)
-                return carry
-
-            lax.fori_loop(0, LINE, own_side, 0)
+            partial[z] = image_block(0, 0, z)
+            near = other(z, 1)
+            strip_wait(near, 1)
+            partial[near] = image_block(0, 0, near)
         else:
-            places = [other(z, step) for step in range(1, LINE)]
-            for place, total in zip(places, image_blocks([(0, side, place) for place in places])):
+            for place, total in zip((z, near), image_blocks([(0, 1, z), (0, 1, near)])):
                 partial[place] += total
 
+    def farther(step, carry):
+        place = other(z, step)
+        strip_wait(place, step)
+        partial[place] = sum(image_blocks([(0, 0, place), (0, 1, place)]))
+        return carry
+
+    lax.fori_loop(2, LINE, farther, 0)
+
+    places = [other(z, step) for step in range(1, LINE)]
     pair.wait_recv()
     relay.start()
     units[1, core] = full[1, core, 0:factors, :].T
@@ -238,7 +240,7 @@
 
     lax.fori_loop(0, LINE - 1, mate_last, 0)
 
-    image = partial[z] + sum(image_blocks([(0, 1, z), (1, 0, z), (1, 1, z)]))
+    image = partial[z] + sum(image_blocks([(1, 0, z), (1, 1, z)]))
     for step in range(1, LINE):
         place = other(z, step)
         remote(

time: 31.4 us -> 31.1 us (level)
  Pallas kernels: 30.7 us -> 30.3 us
    pallas_call x1, Pallas kernels: 30.7 us -> 30.3 us  [fused_per_device(): pl.pallas_call(fused, out_shape=pltpu.VMEM((block, strip), f32), in_specs...]
where the time goes in v8:
time: 31.1 us; the launch traced here: 30.9 us
  Pallas kernels  30.3 us (97%)
  local copies, waits for them, and re-layouts  0.62 us (2%)
    pallas_call x1, Pallas kernels, fused_per_device(): pl.pallas_call(fused, out_shape=pltpu.VMEM((block, strip), f32), in_specs...  30.3 us

profile of v8, /device:TPU:0, one launch (start us, length us, event | category | flops | bytes accessed | tf_op | source)
XLA Modules:
  0.0 30.9 jit_solution(6933894461924340289)
XLA Ops:
  0.0 30.3 %shard_map.46 = f32[16,512]{1,0:T(8,128)S(1)} custom-call(bf16[64,512]{1,0:T(8,128)(2,1)} %bitcast.3, bf16[16,2048]{1,0:T(8,128)(2,1)} %bitcast.4, bf16[4,2048]{1,0:T(4,128)(2,1)} %bitcast.5, f32[1,512]{1,0:T(1,128)} %weight_hbm.1), custom_call_target="tpu_custom_call" | custom-call | flops 1342177280 | bytes 180224 | tf_op jit(solution)/shard_map/pallas_call | solution.py:321
  30.3 0.6 %copy.6 = f32[16,512]{1,0:T(8,128)} copy(f32[16,512]{1,0:T(8,128)S(1)} %shard_map.46) | data formatting | bytes 65536

commit v9 on v8

--- a/solution.py
+++ b/solution.py
@@ -8,7 +8,7 @@
 ROWS = 4
 LINE = 4
 GROUP = 2 * ROWS
-CHUNK = 256
+CHUNK = 512
 LOG2_E = 1.4426950408889634
 
 

time: 31.1 us -> 31.2 us (level)
  no operation moved by 1% of the time
where the time goes in v9:
time: 31.2 us; the launch traced here: 31.1 us
  Pallas kernels  30.5 us (98%)
  local copies, waits for them, and re-layouts  0.62 us (2%)
    pallas_call x1, Pallas kernels, fused_per_device(): pl.pallas_call(fused, out_shape=pltpu.VMEM((block, strip), f32), in_specs...  30.5 us

profile of v9, /device:TPU:0, one launch (start us, length us, event | category | flops | bytes accessed | tf_op | source)
XLA Modules:
  0.0 31.1 jit_solution(12340686387033321369)
XLA Ops:
  0.0 30.5 %shard_map.46 = f32[16,512]{1,0:T(8,128)S(1)} custom-call(bf16[64,512]{1,0:T(8,128)(2,1)} %bitcast.3, bf16[16,2048]{1,0:T(8,128)(2,1)} %bitcast.4, bf16[4,2048]{1,0:T(4,128)(2,1)} %bitcast.5, f32[1,512]{1,0:T(1,128)} %weight_hbm.1), custom_call_target="tpu_custom_call" | custom-call | flops 1342177280 | bytes 180224 | tf_op jit(solution)/shard_map/pallas_call | solution.py:321
  30.5 0.6 %copy.6 = f32[16,512]{1,0:T(8,128)} copy(f32[16,512]{1,0:T(8,128)S(1)} %shard_map.46) | data formatting | bytes 65536

commit v10 on v8

--- a/solution.py
+++ b/solution.py
@@ -159,27 +159,41 @@
         ).wait_recv()
 
     def image_blocks(tasks):
-        steps = [(number, first) for number in range(len(tasks)) for first in range(0, half, CHUNK)]
-        totals = [jnp.zeros((block, strips.shape[2]), jnp.float32) for _ in tasks]
+        wide = strips.shape[2]
+        steps = [
+            (number, first, left)
+            for number in range(len(tasks))
+            for first in range(0, half, CHUNK)
+            for left in range(0, wide, CHUNK)
+        ]
+        totals = {
+            (number, left): jnp.zeros((block, CHUNK), jnp.float32)
+            for number in range(len(tasks))
+            for left in range(0, wide, CHUNK)
+        }
         corr = affinity = None
         for turn in range(len(steps) + 2):
             corr_next = affinity_next = None
             if turn < len(steps):
-                number, first = steps[turn]
+                number, first, left = steps[turn]
                 which, side, place = tasks[number]
                 corr_next = jnp.dot(
-                    units[which, side, first : first + CHUNK, :], strips[place], preferred_element_type=jnp.float32
+                    units[which, side, first : first + CHUNK, :], strips[place, :, left : left + CHUNK],
+                    preferred_element_type=jnp.float32,
                 )
             if corr is not None:
                 affinity_next = jnp.exp2(corr * LOG2_E).astype(jnp.bfloat16)
             if affinity is not None:
-                number, first = steps[turn - 2]
+                number, first, left = steps[turn - 2]
                 which, side, place = tasks[number]
-                totals[number] = totals[number] + jnp.dot(
+                totals[number, left] = totals[number, left] + jnp.dot(
                     full[which, side, factors:, first : first + CHUNK], affinity, preferred_element_type=jnp.float32
                 )
             corr, affinity = corr_next, affinity_next
-        return totals
+        return [
+            jnp.concatenate([totals[number, left] for left in range(0, wide, CHUNK)], axis=1)
+            for number in range(len(tasks))
+        ]
 
     def image_block(which, side, place):
         return image_blocks([(which, side, place)])[0]

time: 31.1 us -> 31.8 us (1.023)
  Pallas kernels: 30.3 us -> 31.1 us
    pallas_call x1, Pallas kernels: 30.3 us -> 31.1 us  [fused_per_device(): pl.pallas_call(fused, out_shape=pltpu.VMEM((block, strip), f32), in_specs...]
where the time goes in v10:
time: 31.8 us; the launch traced here: 31.7 us
  Pallas kernels  31.1 us (98%)
  local copies, waits for them, and re-layouts  0.62 us (2%)
    pallas_call x1, Pallas kernels, fused_per_device(): pl.pallas_call(fused, out_shape=pltpu.VMEM((block, strip), f32), in_specs...  31.1 us

profile of v10, /device:TPU:0, one launch (start us, length us, event | category | flops | bytes accessed | tf_op | source)
XLA Modules:
  0.0 31.7 jit_solution(1079549935491576377)
XLA Ops:
  0.0 31.1 %shard_map.46 = f32[16,512]{1,0:T(8,128)S(1)} custom-call(bf16[64,512]{1,0:T(8,128)(2,1)} %bitcast.3, bf16[16,2048]{1,0:T(8,128)(2,1)} %bitcast.4, bf16[4,2048]{1,0:T(4,128)(2,1)} %bitcast.5, f32[1,512]{1,0:T(1,128)} %weight_hbm.1), custom_call_target="tpu_custom_call" | custom-call | flops 1342177280 | bytes 180224 | tf_op jit(solution)/shard_map/pallas_call | solution.py:335
  31.1 0.6 %copy.6 = f32[16,512]{1,0:T(8,128)} copy(f32[16,512]{1,0:T(8,128)S(1)} %shard_map.46) | data formatting | bytes 65536

commit v11 on v8

--- a/solution.py
+++ b/solution.py
@@ -209,13 +209,12 @@
             for place, total in zip((z, near), image_blocks([(0, 1, z), (0, 1, near)])):
                 partial[place] += total
 
-    def farther(step, carry):
-        place = other(z, step)
-        strip_wait(place, step)
-        partial[place] = sum(image_blocks([(0, 0, place), (0, 1, place)]))
-        return carry
-
-    lax.fori_loop(2, LINE, farther, 0)
+    far = [other(z, step) for step in range(2, LINE)]
+    for number, place in enumerate(far):
+        strip_wait(place, number + 2)
+    totals = image_blocks([(0, side, place) for place in far for side in range(2)])
+    for number, place in enumerate(far):
+        partial[place] = totals[2 * number] + totals[2 * number + 1]
 
     places = [other(z, step) for step in range(1, LINE)]
     pair.wait_recv()
@@ -229,16 +228,13 @@
     remote(full.at[1, last], full.at[1, last], twin_sent, twin_landed, twin, col).wait_recv()
     units[1, last] = full[1, last, 0:factors, :].T
 
-    def mate_last(step, carry):
-        place = other(z, LINE - 1 - step)
-        partial[place] += image_block(1, last, place)
-
+    for place, total in zip(places, image_blocks([(1, last, place) for place in places])):
+        partial[place] += total
+    for step in (3, 2, 1):
+        place = other(z, step)
         remote(
             partial.at[place], arrived.at[z], image_sent.at[step], image_landed.at[z], row, line_col(place)
         ).start()
-        return carry
-
-    lax.fori_loop(0, LINE - 1, mate_last, 0)
 
     image = partial[z] + sum(image_blocks([(1, 0, z), (1, 1, z)]))
     for step in range(1, LINE):
@@ -305,7 +301,7 @@
         copy.wait_send()
     pair.wait_send()
     relay.wait_send()
-    for step in range(LINE - 1):
+    for step in range(1, LINE):
         remote(partial.at[z], arrived.at[z], image_sent.at[step], image_landed.at[z], row, mate).wait_send()
 
 

time: 31.1 us -> 31.7 us (1.019)
  Pallas kernels: 30.3 us -> 30.9 us
    pallas_call x1, Pallas kernels: 30.3 us -> 30.9 us  [fused_per_device(): pl.pallas_call(fused, out_shape=pltpu.VMEM((block, strip), f32), in_specs...]
where the time goes in v11:
time: 31.7 us; the launch traced here: 31.6 us
  Pallas kernels  30.9 us (97%)
  local copies, waits for them, and re-layouts  0.62 us (2%)
    pallas_call x1, Pallas kernels, fused_per_device(): pl.pallas_call(fused, out_shape=pltpu.VMEM((block, strip), f32), in_specs...  30.9 us

profile of v11, /device:TPU:0, one launch (start us, length us, event | category | flops | bytes accessed | tf_op | source)
XLA Modules:
  0.0 31.6 jit_solution(14324477457389930975)
XLA Ops:
  0.0 30.9 %shard_map.46 = f32[16,512]{1,0:T(8,128)S(1)} custom-call(bf16[64,512]{1,0:T(8,128)(2,1)} %bitcast.3, bf16[16,2048]{1,0:T(8,128)(2,1)} %bitcast.4, bf16[4,2048]{1,0:T(4,128)(2,1)} %bitcast.5, f32[1,512]{1,0:T(1,128)} %weight_hbm.1), custom_call_target="tpu_custom_call" | custom-call | flops 1342177280 | bytes 180224 | tf_op jit(solution)/shard_map/pallas_call | solution.py:317
  31.0 0.6 %copy.6 = f32[16,512]{1,0:T(8,128)} copy(f32[16,512]{1,0:T(8,128)S(1)} %shard_map.46) | data formatting | bytes 65536
